TPU v7x, 32 devices: a whole 2x2x4 slice. The times are simulated.
32 devices in a mesh: grid: 2 (over x), rank: 4 (over y, core), term: 4 (over z).
Axes of the slice: x: 2, y: 2, z: 4, core: 2. Of those that a mesh axis runs over, the one named last changes fastest.
Arguments:
- rhs: float32 [128, 4, 256], P('rank', 'grid')
- coef: float32 [12, 4, 256], P('term', 'grid'), may hold values from 0.03 to 0.3
- env: float32 [12, 128, 128], P('term', 'rank'), as said below
Outputs:
- solution: float32 [128, 4, 256], P('rank', 'grid')
- residual: float32 [128, 4, 256], P('rank', 'grid')
Inputs may be any that keep to these rules, and one draw needn't show every extreme that they name: env[k] is a symmetric matrix for every k.
All inputs are finite; a program needn't handle non-finite values.
Results may differ from a plain program's by a relative error of at most 0.0003.
Values sent between devices are 32-bit elements; how exact they have to be, the bound alone decides.
A program may use at most 64 MiB of HBM per device.

v0:
```python
import jax
import jax.numpy as jnp
from jax import lax
from jax.sharding import PartitionSpec as P

ITERS = 4


def padded_2(block, sides, width):
    for axis, dim in sides:
        count = lax.axis_size(axis)
        forward = [(i, i + 1) for i in range(count - 1)]
        backward = [(target, source) for source, target in forward]
        low = lax.ppermute(
            lax.slice_in_dim(block, block.shape[dim] - width, None, axis=dim), axis, forward
        )
        high = lax.ppermute(lax.slice_in_dim(block, 0, width, axis=dim), axis, backward)
        block = jnp.concatenate([low, block, high], axis=dim)
    return block


def face_weights(padded):
    wide = jnp.pad(padded, ((0, 0), (0, 0), (1, 1)))
    centre = wide[:, 1:-1, 1:-1]
    face_up = 0.5 * (centre + wide[:, 2:, 1:-1])
    face_down = 0.5 * (centre + wide[:, :-2, 1:-1])
    face_right = 0.5 * (centre + wide[:, 1:-1, 2:])
    face_left = 0.5 * (centre + wide[:, 1:-1, :-2])
    return (face_up + face_down + face_right + face_left, face_up, face_down, face_right, face_left)


def apply_faces(field, faces):
    middle = field[..., 1:-1, :]
    sideways = jnp.pad(middle, [(0, 0)] * (middle.ndim - 1) + [(1, 1)])
    total, face_up, face_down, face_right, face_left = faces
    return (
        total * middle
        - face_up * field[..., 2:, :]
        - face_down * field[..., :-2, :]
        - face_right * sideways[..., 2:]
        - face_left * sideways[..., :-2]
    )


def shards(rhs, coef, env):
    coef_padded = padded_2(coef, (("grid", 1),), 1)
    faces = tuple((weights[:, None] for weights in face_weights(coef_padded)))

    def square_sum(vector):
        return lax.psum(jnp.sum(vector * vector), ("grid", "rank"))

    solution = jnp.zeros(rhs.shape, jnp.float32)
    residual = rhs
    direction = rhs
    norm_now = square_sum(residual)
    for step in range(ITERS):
        padded = padded_2(direction, (("grid", 1),), 1)
        stenciled = apply_faces(padded[None], faces)
        image = lax.psum_scatter(
            jnp.einsum("krs,krxy->sxy", env, stenciled, precision=lax.Precision.HIGHEST),
            "rank",
            scatter_dimension=0,
            tiled=True,
        )
        image = lax.psum(image, "term")
        alpha = norm_now / lax.psum(jnp.sum(direction * image), ("grid", "rank"))
        solution = solution + alpha * direction
        residual = residual - alpha * image
        norm_next = square_sum(residual)
        direction = residual + norm_next / norm_now * direction
        norm_now = norm_next
    return (solution, residual)


def solution(mesh):
    placed = (P("rank", "grid", None), P("term", "grid", None), P("term", "rank", None))
    return jax.shard_map(
        shards,
        mesh=mesh,
        in_specs=placed,
        out_specs=(P("rank", "grid", None), P("rank", "grid", None)),
        check_vma=False,
    )
```

profile of v0, /device:TPU:0, one launch (start us, length us, event | category | flops | bytes accessed | tf_op | source)
XLA Modules:
  0.0 443.1 jit_solution(13769848011755938709)
XLA Ops:
  7.2 0.8 fusion.103
  8.0 4.8 %collective-permute-start.1 = (f32[3,1,256]{2,1,0:T(1,128)S(1)}, f32[3,1,256]{2,1,0:T(1,128)S(1)}, u32[]{:S(2)}, u32[]{:S(2)}) collective-permute-start(f32[3,1,256]{2,1,0:T(1,128)S(1)} %get-tuple-element.49), channel_id=1, source_target_pairs={{0,16},{1,17},{2,18},{3,19},{4,20},{5,21},{6,22},{7,23},{8,24},{9,... | collective-permute-start | bytes 9224 | tf_op jit(solution)/shard_map/ppermute | solution.py:14
  12.8 1.3 collective-permute-start
  14.2 1.0 fusion.102
  15.1 4.5 %collective-permute-start.2 = (f32[32,1,256]{2,1,0:T(1,128)S(1)}, f32[32,1,256]{2,1,0:T(1,128)S(1)}, u32[]{:S(2)}, u32[]{:S(2)}) collective-permute-start(f32[32,1,256]{2,1,0:T(1,128)S(1)} %get-tuple-element.47), channel_id=1, source_target_pairs={{0,16},{1,17},{2,18},{3,19},{4,20},{5,21},{6,22},{7,23},{8,24},{9,... | collective-permute-start | bytes 98312 | tf_op jit(solution)/shard_map/ppermute | solution.py:14
  19.7 1.3 collective-permute-start.3
  21.3 4.2 collective-permute-done.3
  26.6 0.8 copy.46
  27.5 0.6 copy-done.7
  29.4 30.5 %all-reduce.27.cloned.1.call-done = f32[128,2,256]{2,1,0:T(2,128)} async-done(((f32[128,2,256]{2,1,0:T(2,128)}), f32[128,2,256]{2,1,0:T(2,128)}) %all-reduce.27.cloned.1.call-update) | async-done | bytes 262160
  59.9 1.5 constant_dynamic-slice_fusion.3
  61.4 35.5 %all-reduce.19.cloned.1.call-done = f32[32,2,256]{2,1,0:T(2,128)} async-done(((f32[32,2,256]{2,1,0:T(2,128)}), f32[32,2,256]{2,1,0:T(2,128)}) %all-reduce.19.cloned.1.call-update) | async-done | bytes 65552 | tf_op jit(solution)/shard_map/psum | solution.py:65
  96.9 1.6 multiply_reduce_fusion.6
  98.5 12.5 %all-reduce.9 = (f32[]{:T(128)}, f32[]{:T(128)}) all-reduce(f32[]{:T(128)} %get-tuple-element.5, f32[]{:T(128)} %get-tuple-element.4), channel_id=1, replica_groups=mesh['grid'=2,'rank'=4,'term'=4] {'grid','rank'}, use_global_device_ids=true, to_apply=%region_1.2 | all-reduce | flops 2 | bytes 16 | tf_op jit(solution)/shard_map/psum | solution.py:50
  112.3 0.7 multiply_reduce_fusion.5
  113.0 12.5 %psum.87 = f32[]{:T(128)} all-reduce(f32[]{:T(128)} %multiply_reduce_fusion.5), channel_id=1, replica_groups=mesh['grid'=2,'rank'=4,'term'=4] {'grid','rank'}, use_global_device_ids=true, to_apply=%region_7.8 | all-reduce | flops 1 | bytes 8 | tf_op jit(solution)/shard_map/psum | solution.py:50
  126.9 3.4 collective-permute-start.4
  130.3 1.3 collective-permute-start.5
  131.9 4.2 collective-permute-done.5
  136.9 0.8 copy.50
  137.8 30.0 %all-reduce.29.cloned.1.call-done = f32[128,2,256]{2,1,0:T(2,128)} async-done(((f32[128,2,256]{2,1,0:T(2,128)}), f32[128,2,256]{2,1,0:T(2,128)}) %all-reduce.29.cloned.1.call-update) | async-done | bytes 262160
  167.8 1.5 constant_dynamic-slice_fusion.2
  169.3 35.3 %all-reduce.21.cloned.1.call-done = f32[32,2,256]{2,1,0:T(2,128)} async-done(((f32[32,2,256]{2,1,0:T(2,128)}), f32[32,2,256]{2,1,0:T(2,128)}) %all-reduce.21.cloned.1.call-update) | async-done | bytes 65552 | tf_op jit(solution)/shard_map/psum | solution.py:65
  204.6 1.6 multiply_reduce_fusion.4
  206.2 12.5 %psum.89 = f32[]{:T(128)} all-reduce(f32[]{:T(128)} %multiply_reduce_fusion.4), channel_id=1, replica_groups=mesh['grid'=2,'rank'=4,'term'=4] {'grid','rank'}, use_global_device_ids=true, to_apply=%region_11.12 | all-reduce | flops 1 | bytes 8 | tf_op jit(solution)/shard_map/psum | solution.py:66
  220.1 0.7 multiply_reduce_fusion.3
  220.7 12.4 %psum.90 = f32[]{:T(128)} all-reduce(f32[]{:T(128)} %get-tuple-element.10), channel_id=1, replica_groups=mesh['grid'=2,'rank'=4,'term'=4] {'grid','rank'}, use_global_device_ids=true, to_apply=%region_13.14 | all-reduce | flops 1 | bytes 8 | tf_op jit(solution)/shard_map/psum | solution.py:50
  234.6 3.4 collective-permute-start.6
  238.0 1.3 collective-permute-start.7
  239.6 4.2 collective-permute-done.7
  244.6 0.8 copy.54
  245.5 30.0 %all-reduce.31.cloned.1.call-done = f32[128,2,256]{2,1,0:T(2,128)} async-done(((f32[128,2,256]{2,1,0:T(2,128)}), f32[128,2,256]{2,1,0:T(2,128)}) %all-reduce.31.cloned.1.call-update) | async-done | bytes 262160
  275.4 1.5 constant_dynamic-slice_fusion.1
  277.0 35.3 %all-reduce.23.cloned.1.call-done = f32[32,2,256]{2,1,0:T(2,128)} async-done(((f32[32,2,256]{2,1,0:T(2,128)}), f32[32,2,256]{2,1,0:T(2,128)}) %all-reduce.23.cloned.1.call-update) | async-done | bytes 65552 | tf_op jit(solution)/shard_map/psum | solution.py:65
  312.3 1.6 multiply_reduce_fusion.2
  313.9 12.5 %psum.92 = f32[]{:T(128)} all-reduce(f32[]{:T(128)} %multiply_reduce_fusion.2), channel_id=1, replica_groups=mesh['grid'=2,'rank'=4,'term'=4] {'grid','rank'}, use_global_device_ids=true, to_apply=%region_17.18 | all-reduce | flops 1 | bytes 8 | tf_op jit(solution)/shard_map/psum | solution.py:66
  327.7 0.7 multiply_reduce_fusion.1
  328.4 12.5 %psum.93 = f32[]{:T(128)} all-reduce(f32[]{:T(128)} %get-tuple-element.8), channel_id=1, replica_groups=mesh['grid'=2,'rank'=4,'term'=4] {'grid','rank'}, use_global_device_ids=true, to_apply=%region_19.20 | all-reduce | flops 1 | bytes 8 | tf_op jit(solution)/shard_map/psum | solution.py:50
  342.3 3.4 collective-permute-start.8
  345.7 1.3 collective-permute-start.9
  347.3 4.2 collective-permute-done.9
  352.3 0.8 copy.58
  353.2 30.0 %all-reduce.33.cloned.1.call-done = f32[128,2,256]{2,1,0:T(2,128)} async-done(((f32[128,2,256]{2,1,0:T(2,128)}), f32[128,2,256]{2,1,0:T(2,128)}) %all-reduce.33.cloned.1.call-update) | async-done | bytes 262160
  383.1 1.5 constant_dynamic-slice_fusion
  384.6 35.5 %all-reduce.25.cloned.1.call-done = f32[32,2,256]{2,1,0:T(2,128)} async-done(((f32[32,2,256]{2,1,0:T(2,128)}), f32[32,2,256]{2,1,0:T(2,128)}) %all-reduce.25.cloned.1.call-update) | async-done | bytes 65552 | tf_op jit(solution)/shard_map/psum | solution.py:65
  420.1 1.6 multiply_reduce_fusion
  421.7 12.5 %psum.95 = f32[]{:T(128)} all-reduce(f32[]{:T(128)} %multiply_reduce_fusion), channel_id=1, replica_groups=mesh['grid'=2,'rank'=4,'term'=4] {'grid','rank'}, use_global_device_ids=true, to_apply=%region_23.24 | all-reduce | flops 1 | bytes 8 | tf_op jit(solution)/shard_map/psum | solution.py:66
  435.6 0.7 multiply_subtract_fusion
  (81 shorter events, 5.6 us)
Async XLA Ops:
  7.2 18.8 %copy-start = (f32[3,32,128]{2,1,0:T(8,128)S(1)}, f32[3,32,128]{2,1,0:T(8,128)}, u32[]{:S(2)}) copy-start(f32[3,32,128]{2,1,0:T(8,128)} %param.5) | copy-start | bytes 147460
  7.2 52.7 %all-reduce.27.cloned.1.call-start = ((), (), s32[]{:S(2)}) async-start(), calls=%async_computation.4 | async-start | bytes 524288
  8.0 13.0 %collective-permute-start.1 = (f32[3,1,256]{2,1,0:T(1,128)S(1)}, f32[3,1,256]{2,1,0:T(1,128)S(1)}, u32[]{:S(2)}, u32[]{:S(2)}) collective-permute-start(f32[3,1,256]{2,1,0:T(1,128)S(1)} %get-tuple-element.49), channel_id=1, source_target_pairs={{0,16},{1,17},{2,18},{3,19},{4,20},{5,21},{6,22},{7,23},{8,24},{9,... | collective-permute-start | bytes 9224 | tf_op jit(solution)/shard_map/ppermute | solution.py:14
  12.8 8.2 %collective-permute-start = (f32[3,1,256]{2,1,0:T(1,128)S(1)}, f32[3,1,256]{2,1,0:T(1,128)S(1)}, u32[]{:S(2)}, u32[]{:S(2)}) collective-permute-start(f32[3,1,256]{2,1,0:T(1,128)S(1)} %get-tuple-element.50), channel_id=1, source_target_pairs={{16,0},{17,1},{18,2},{19,3},{20,4},{21,5},{22,6},{23,7},{24,8},{25... | collective-permute-start | bytes 9224 | tf_op jit(solution)/shard_map/ppermute | solution.py:17
  14.1 6.9 %copy-start.6 = (f32[3,2,256]{2,1,0:T(2,128)S(1)}, f32[3,2,256]{2,1,0:T(2,128)}, u32[]{:S(2)}) copy-start(f32[3,2,256]{2,1,0:T(2,128)} %param.4) | copy-start | bytes 18436
  15.1 6.1 %collective-permute-start.2 = (f32[32,1,256]{2,1,0:T(1,128)S(1)}, f32[32,1,256]{2,1,0:T(1,128)S(1)}, u32[]{:S(2)}, u32[]{:S(2)}) collective-permute-start(f32[32,1,256]{2,1,0:T(1,128)S(1)} %get-tuple-element.47), channel_id=1, source_target_pairs={{0,16},{1,17},{2,18},{3,19},{4,20},{5,21},{6,22},{7,23},{8,24},{9,... | collective-permute-start | bytes 98312 | tf_op jit(solution)/shard_map/ppermute | solution.py:14
  19.7 5.8 %collective-permute-start.3 = (f32[32,1,256]{2,1,0:T(1,128)S(1)}, f32[32,1,256]{2,1,0:T(1,128)S(1)}, u32[]{:S(2)}, u32[]{:S(2)}) collective-permute-start(f32[32,1,256]{2,1,0:T(1,128)S(1)} %get-tuple-element.48), channel_id=1, source_target_pairs={{16,0},{17,1},{18,2},{19,3},{20,4},{21,5},{22,6},{23,7},{24,8},{25... | collective-permute-start | bytes 98312 | tf_op jit(solution)/shard_map/ppermute | solution.py:17
  21.1 4.4 copy-start.1
  27.4 69.5 %all-reduce.19.cloned.1.call-start = ((), (), s32[]{:S(2)}) async-start(), calls=%async_computation | async-start | bytes 131072 | tf_op jit(solution)/shard_map/psum | solution.py:65
  27.5 0.7 copy-start.7
  61.4 106.4 %all-reduce.29.cloned.1.call-start = ((), (), s32[]{:S(2)}) async-start(), calls=%async_computation.5 | async-start | bytes 524288
  96.9 15.4 %copy-start.2 = (f32[32,2,256]{2,1,0:T(2,128)S(1)}, f32[32,2,256]{2,1,0:T(2,128)}, u32[]{:S(2)}) copy-start(f32[32,2,256]{2,1,0:T(2,128)} %all-reduce.19.cloned.1.call-done) | copy-start | bytes 196612
  126.9 4.9 %collective-permute-start.4 = (f32[32,1,256]{2,1,0:T(1,128)S(1)}, f32[32,1,256]{2,1,0:T(1,128)S(1)}, u32[]{:S(2)}, u32[]{:S(2)}) collective-permute-start(f32[32,1,256]{2,1,0:T(1,128)S(1)} %get-tuple-element.43), channel_id=1, source_target_pairs={{0,16},{1,17},{2,18},{3,19},{4,20},{5,21},{6,22},{7,23},{8,24},{9,... | collective-permute-start | bytes 98312 | tf_op jit(solution)/shard_map/ppermute | solution.py:14
  130.3 5.8 %collective-permute-start.5 = (f32[32,1,256]{2,1,0:T(1,128)S(1)}, f32[32,1,256]{2,1,0:T(1,128)S(1)}, u32[]{:S(2)}, u32[]{:S(2)}) collective-permute-start(f32[32,1,256]{2,1,0:T(1,128)S(1)} %get-tuple-element.44), channel_id=1, source_target_pairs={{16,0},{17,1},{18,2},{19,3},{20,4},{21,5},{22,6},{23,7},{24,8},{25... | collective-permute-start | bytes 98312 | tf_op jit(solution)/shard_map/ppermute | solution.py:17
  137.7 66.9 %all-reduce.21.cloned.1.call-start = ((), (), s32[]{:S(2)}) async-start(), calls=%async_computation.1 | async-start | bytes 131072 | tf_op jit(solution)/shard_map/psum | solution.py:65
  169.2 106.2 %all-reduce.31.cloned.1.call-start = ((), (), s32[]{:S(2)}) async-start(), calls=%async_computation.6 | async-start | bytes 524288
  204.6 15.4 %copy-start.4 = (f32[32,2,256]{2,1,0:T(2,128)S(1)}, f32[32,2,256]{2,1,0:T(2,128)}, u32[]{:S(2)}) copy-start(f32[32,2,256]{2,1,0:T(2,128)} %all-reduce.21.cloned.1.call-done) | copy-start | bytes 196612
  234.6 4.9 %collective-permute-start.6 = (f32[32,1,256]{2,1,0:T(1,128)S(1)}, f32[32,1,256]{2,1,0:T(1,128)S(1)}, u32[]{:S(2)}, u32[]{:S(2)}) collective-permute-start(f32[32,1,256]{2,1,0:T(1,128)S(1)} %get-tuple-element.39), channel_id=1, source_target_pairs={{0,16},{1,17},{2,18},{3,19},{4,20},{5,21},{6,22},{7,23},{8,24},{9,... | collective-permute-start | bytes 98312 | tf_op jit(solution)/shard_map/ppermute | solution.py:14
  238.0 5.8 %collective-permute-start.7 = (f32[32,1,256]{2,1,0:T(1,128)S(1)}, f32[32,1,256]{2,1,0:T(1,128)S(1)}, u32[]{:S(2)}, u32[]{:S(2)}) collective-permute-start(f32[32,1,256]{2,1,0:T(1,128)S(1)} %get-tuple-element.40), channel_id=1, source_target_pairs={{16,0},{17,1},{18,2},{19,3},{20,4},{21,5},{22,6},{23,7},{24,8},{25... | collective-permute-start | bytes 98312 | tf_op jit(solution)/shard_map/ppermute | solution.py:17
  245.4 66.9 %all-reduce.23.cloned.1.call-start = ((), (), s32[]{:S(2)}) async-start(), calls=%async_computation.2 | async-start | bytes 131072 | tf_op jit(solution)/shard_map/psum | solution.py:65
  276.9 106.2 %all-reduce.33.cloned.1.call-start = ((), (), s32[]{:S(2)}) async-start(), calls=%async_computation.7 | async-start | bytes 524288
  312.3 15.4 %copy-start.3 = (f32[32,2,256]{2,1,0:T(2,128)S(1)}, f32[32,2,256]{2,1,0:T(2,128)}, u32[]{:S(2)}) copy-start(f32[32,2,256]{2,1,0:T(2,128)} %all-reduce.23.cloned.1.call-done) | copy-start | bytes 196612
  342.3 4.9 %collective-permute-start.8 = (f32[32,1,256]{2,1,0:T(1,128)S(1)}, f32[32,1,256]{2,1,0:T(1,128)S(1)}, u32[]{:S(2)}, u32[]{:S(2)}) collective-permute-start(f32[32,1,256]{2,1,0:T(1,128)S(1)} %get-tuple-element.35), channel_id=1, source_target_pairs={{0,16},{1,17},{2,18},{3,19},{4,20},{5,21},{6,22},{7,23},{8,24},{9,... | collective-permute-start | bytes 98312 | tf_op jit(solution)/shard_map/ppermute | solution.py:14
  345.7 5.8 %collective-permute-start.9 = (f32[32,1,256]{2,1,0:T(1,128)S(1)}, f32[32,1,256]{2,1,0:T(1,128)S(1)}, u32[]{:S(2)}, u32[]{:S(2)}) collective-permute-start(f32[32,1,256]{2,1,0:T(1,128)S(1)} %get-tuple-element.36), channel_id=1, source_target_pairs={{16,0},{17,1},{18,2},{19,3},{20,4},{21,5},{22,6},{23,7},{24,8},{25... | collective-permute-start | bytes 98312 | tf_op jit(solution)/shard_map/ppermute | solution.py:17
  353.1 67.0 %all-reduce.25.cloned.1.call-start = ((), (), s32[]{:S(2)}) async-start(), calls=%async_computation.3 | async-start | bytes 131072 | tf_op jit(solution)/shard_map/psum | solution.py:65
  420.1 15.4 %copy-start.5 = (f32[32,2,256]{2,1,0:T(2,128)S(1)}, f32[32,2,256]{2,1,0:T(2,128)}, u32[]{:S(2)}) copy-start(f32[32,2,256]{2,1,0:T(2,128)} %all-reduce.25.cloned.1.call-done) | copy-start | bytes 196612
Sparse Core Ops, SparseCore 0:
  27.6 32.2 all-reduce.26
  62.9 33.9 all-reduce.18
  137.9 29.8 all-reduce.28
  170.6 33.9 all-reduce.20
  245.5 29.8 all-reduce.30
  278.3 33.9 all-reduce.22
  353.2 29.8 all-reduce.32
  386.1 33.9 all-reduce.24
where the time goes:
time: 444 us; the launch traced here: 443 us
  waiting for transfers between devices  280 us (63%)
  blocking collectives  87.3 us (20%)
  starting transfers between devices  26.2 us (6%)
  between operations  24.8 us (6%)
  local copies, waits for them, and re-layouts  13.1 us (3%)
  other arithmetic  9.37 us (2%)
    psum x4, waiting for transfers between devices, shards(): image = lax.psum(image, 'term')  142 us
    unnamed x12, waiting for transfers between devices  121 us
    psum x4, blocking collectives, square_sum(): return lax.psum(jnp.sum(vector * vector), ('grid', 'rank'))  49.9 us
    psum x3, blocking collectives, shards(): alpha = norm_now / lax.psum(jnp.sum(direction * image), ('grid', 'rank'))  37.4 us
    ppermute x5, starting transfers between devices, padded_2(): lax.ppermute(lax.slice_in_dim(block, block.shape[dim] - width, None, axis...  19.4 us
    ppermute x5, waiting for transfers between devices, padded_2(): lax.ppermute(lax.slice_in_dim(block, 0, width, axis=dim), axis, backward)  16.9 us
  transfers between devices with their start and end apart: 18, of which 15 were waited for; matrix products, arithmetic and copies ran while one was open for 0% of the time, Pallas kernels for 0%

commit v1 on v0

--- a/solution.py
+++ b/solution.py
@@ -1,9 +1,14 @@
+import functools
+
 import jax
 import jax.numpy as jnp
 from jax import lax
+from jax.experimental import pallas as pl
+from jax.experimental.pallas import tpu as pltpu
 from jax.sharding import PartitionSpec as P
 
 ITERS = 4
+MESH = pl.DeviceIdType.MESH
 
 
 def padded_2(block, sides, width):
@@ -72,10 +77,296 @@
     return (solution, residual)
 
 
+def shift_sum(v):
+    lane = lax.broadcasted_iota(jnp.int32, v.shape, v.ndim - 1)
+    n = v.shape[-1]
+    axis = v.ndim - 1
+    left = jnp.where(lane == 0, 0.0, pltpu.roll(v, 1, axis))
+    right = jnp.where(lane == n - 1, 0.0, pltpu.roll(v, n - 1, axis))
+    return left + right
+
+
+def neighbours(read, x, count):
+    total = shift_sum(read(x))
+    if x > 0:
+        total = total + read(x - 1)
+    if x < count - 1:
+        total = total + read(x + 1)
+    return total
+
+
+def split3(v):
+    high = v.astype(jnp.bfloat16)
+    low = (v - high.astype(jnp.float32)).astype(jnp.bfloat16)
+    return jnp.concatenate([high, high, low], axis=0)
+
+
+def total_sum(v):
+    return jnp.sum(v, axis=(0, 1), keepdims=True)
+
+
+def cg_kernel(
+    sizes,
+    rhs_ref, coef_ref, env_ref,
+    sol_ref, out_ref,
+    env_all, coef_all, coef_tab, diag_tab, stack, residual, direction, image, partial, weighted, dots,
+    rhs_send, rhs_recv, sib_send, sib_recv, env_send, env_recv, envy_send, envy_recv,
+    coef_send, coef_recv, img_send, img_recv, dot_send, dot_recv,
+):
+    grids, ys, terms, per, rows, strip, ny, ranks = sizes
+    nx = grids * strip
+    half = ys * rows
+    gx = lax.axis_index("grid")
+    rank = lax.axis_index("rank")
+    gz = lax.axis_index("term")
+    gy = rank // 2
+    core = rank % 2
+    sibling = (gx, gy * 2 + (1 - core), gz)
+
+    def at(dx, dy, dz):
+        return ((gx + dx) % grids, ((gy + dy) % ys) * 2 + core, (gz + dz) % terms)
+
+    peers = [at(dx, 0, dz) for dx in range(grids) for dz in range(terms) if dx or dz]
+    peers += [at(dx, dy, 0) for dx in range(grids) for dy in range(1, ys)]
+    peers.append(sibling)
+    barrier = pltpu.get_barrier_semaphore()
+    for peer in peers:
+        pl.semaphore_signal(barrier, inc=1, device_id=peer, device_id_type=MESH)
+
+    for i in range(strip):
+        residual[gx * strip + i, gy, core] = rhs_ref[:, i, :]
+    env_all[gz, :, gy] = env_ref[...]
+    coef_all[gz, gx] = coef_ref[...]
+    pl.semaphore_wait(barrier, len(peers))
+
+    def remote(src, dst, send, recv, device):
+        copy = pltpu.make_async_remote_copy(
+            src_ref=src, dst_ref=dst, send_sem=send, recv_sem=recv, device_id=device, device_id_type=MESH
+        )
+        return copy
+
+    def block_of(dx, dy, which):
+        return residual.at[pl.ds(((gx + dx) % grids) * strip, strip), (gy + dy) % ys, which]
+
+    own = block_of(0, 0, core)
+    env_copies, envy_copies, rhs_copies, sib_copies, coef_copies = {}, {}, {}, {}, {}
+    order = [1, terms - 1] + list(range(2, terms - 1))
+    for dz in order:
+        copy = remote(env_ref, env_all.at[gz, :, gy], env_send.at[dz], env_recv.at[dz], at(0, 0, dz))
+        copy.start()
+        env_copies[dz] = copy
+    for dx in range(grids):
+        for dy in range(ys):
+            if dx or dy:
+                d = dx * ys + dy
+                copy = remote(own, own, rhs_send.at[d], rhs_recv.at[d], at(dx, dy, 0))
+                copy.start()
+                rhs_copies[d] = copy
+    envy_copies[0] = remote(env_ref, env_all.at[gz, :, gy], envy_send.at[0], envy_recv.at[0], at(0, 1, 0))
+    envy_copies[0].start()
+    for dx in range(grids):
+        for dz in range(terms):
+            if dx or dz:
+                d = dx * terms + dz
+                copy = remote(coef_ref, coef_all.at[gz, gx], coef_send.at[d], coef_recv.at[d], at(dx, 0, dz))
+                copy.start()
+                coef_copies[d] = copy
+
+    def to_sibling(dx, dy):
+        d = dx * ys + dy
+        block = block_of(dx, dy, core)
+        copy = remote(block, block, sib_send.at[d], sib_recv.at[d], sibling)
+        copy.start()
+        sib_copies[d] = copy
+
+    to_sibling(0, 0)
+    for dx in range(grids):
+        for dy in range(ys):
+            if dx or dy:
+                rhs_copies[dx * ys + dy].wait_recv()
+                to_sibling(dx, dy)
+    for dz in order:
+        env_copies[dz].wait_recv()
+        block = env_all.at[(gz - dz + terms) % terms, :, gy]
+        copy = remote(block, block, envy_send.at[dz], envy_recv.at[dz], at(0, 1, 0))
+        copy.start()
+        envy_copies[dz] = copy
+
+    for copy in coef_copies.values():
+        copy.wait_recv()
+    for x in range(nx):
+        for z in range(terms):
+            for i in range(per):
+                k = z * per + i
+                coef_tab[x, k : k + 1, :] = coef_all[z, x // strip, i, x % strip : x % strip + 1, :]
+    for x in range(nx):
+        diag_tab[x] = 0.5 * neighbours(lambda j: coef_tab[j], x, nx)
+
+    for copy in sib_copies.values():
+        copy.wait_recv()
+    square = jnp.zeros((ranks, ny), jnp.float32)
+    for x in range(nx):
+        field = residual[x].reshape(ranks, ny)
+        direction[x] = field
+        square = square + field * field
+    norm_now = total_sum(square)
+
+    for copy in envy_copies.values():
+        copy.wait_recv()
+    for z in range(terms):
+        for i in range(per):
+            k = z * per + i
+            block = env_all[z, i].reshape(half, ranks)
+            high = block.astype(jnp.bfloat16)
+            low = (block - high.astype(jnp.float32)).astype(jnp.bfloat16)
+            stack[pl.ds(k * half, half), 0:ranks] = high
+            stack[pl.ds(k * half, half), ranks : 2 * ranks] = low
+            stack[pl.ds(k * half, half), 2 * ranks : 3 * ranks] = high
+    for copies in (env_copies, envy_copies, rhs_copies, sib_copies, coef_copies):
+        for copy in copies.values():
+            copy.wait_send()
+
+    count = terms * per
+
+    def product(x):
+        field = direction[x]
+        wide = 2.0 * field - 0.5 * neighbours(lambda j: direction[j], x, nx)
+        plain = jnp.dot(stack[...], split3(field), preferred_element_type=jnp.float32)
+        spread = jnp.dot(stack[...], split3(wide), preferred_element_type=jnp.float32)
+        total = jnp.zeros((half, ny), jnp.float32)
+        inner = jnp.zeros((half, ny), jnp.float32)
+        for k in range(count):
+            c = coef_tab[x, k : k + 1, :]
+            d = diag_tab[x, k : k + 1, :]
+            u = plain[k * half : (k + 1) * half]
+            total = total + c * spread[k * half : (k + 1) * half] + d * u
+            inner = inner + c * u
+        partial[x] = total
+        weighted[x] = inner
+
+    def finish(x, slot):
+        value = partial[x] - 0.5 * neighbours(lambda j: weighted[j], x, nx)
+        image[slot, x, :, core] = value.reshape(ys, rows, ny)
+
+    def image_copy(x, slot):
+        block = image.at[slot, x, :, core]
+        return remote(block, block, img_send.at[slot, x], img_recv.at[slot, x], sibling)
+
+    def operate(slot, send):
+        for x in range(nx + 1):
+            if x < nx:
+                product(x)
+            if x > 0:
+                finish(x - 1, slot)
+                if send:
+                    image_copy(x - 1, slot).start()
+
+    strips = pl.ds(gx * strip, strip)
+
+    def iteration(step, norm_now):
+        slot = step % 2
+        operate(slot, True)
+        product_sum = jnp.zeros((ranks, ny), jnp.float32)
+        for x in range(nx):
+            image_copy(x, slot).wait_recv()
+            product_sum = product_sum + direction[x] * image[slot, x].reshape(ranks, ny)
+        alpha = norm_now / total_sum(product_sum)
+        square = jnp.zeros((ranks, ny), jnp.float32)
+        for x in range(nx):
+            fresh = residual[x].reshape(ranks, ny) - alpha * image[slot, x].reshape(ranks, ny)
+            residual[x] = fresh.reshape(ys, 2, rows, ny)
+            square = square + fresh * fresh
+        norm_next = total_sum(square)
+        beta = norm_next / norm_now
+        mine = pl.ds(pl.multiple_of(rank * rows, rows), rows)
+        for i in range(strip):
+            sol_ref[i] = sol_ref[i] + alpha * direction[gx * strip + i, mine, :]
+        for x in range(nx):
+            direction[x] = residual[x].reshape(ranks, ny) + beta * direction[x]
+        for x in range(nx):
+            image_copy(x, slot).wait_send()
+        return norm_next
+
+    sol_ref[...] = jnp.zeros_like(sol_ref)
+    norm_now = lax.fori_loop(0, ITERS - 1, iteration, norm_now)
+
+    slot = (ITERS - 1) % 2
+    operate(slot, False)
+    mine = pl.ds(pl.multiple_of(rank * rows, rows), rows)
+    part = jnp.zeros((rows, ny), jnp.float32)
+    for x in range(nx):
+        for y in range(ys):
+            field = direction[x, pl.ds(pl.multiple_of((y * 2 + core) * rows, rows), rows), :]
+            part = part + field * image[slot, x, y, core]
+    dots[core] = jnp.broadcast_to(total_sum(part), (8, 128))
+    copy = remote(dots.at[core], dots.at[core], dot_send, dot_recv, sibling)
+    copy.start()
+    copy.wait()
+    both = dots[0] + dots[1]
+    alpha = norm_now / both[0:1, 0:1]
+    for i in range(strip):
+        x = gx * strip + i
+        sol_ref[i] = sol_ref[i] + alpha * direction[x, mine, :]
+        out_ref[i] = residual[x, gy, core] - alpha * image[slot, x, gy, core]
+
+
+def fused(mesh, rhs, coef, env):
+    grids, rank_shards, terms = (mesh.shape[a] for a in ("grid", "rank", "term"))
+    ys = rank_shards // 2
+    rows, strip, ny = rhs.shape
+    per, ranks = env.shape[0], env.shape[2]
+    nx, half, count = grids * strip, ys * rows, per * terms
+    sizes = (grids, ys, terms, per, rows, strip, ny, ranks)
+    f32 = jnp.float32
+    dma = pltpu.SemaphoreType.DMA
+    block = jax.ShapeDtypeStruct((strip, rows, ny), f32)
+    sol, res = pl.pallas_call(
+        functools.partial(cg_kernel, sizes),
+        out_shape=(block, block),
+        in_specs=[pl.BlockSpec(memory_space=pltpu.VMEM)] * 3,
+        out_specs=(pl.BlockSpec(memory_space=pltpu.VMEM),) * 2,
+        scratch_shapes=[
+            pltpu.VMEM((terms, per, ys, rows, ranks), f32),
+            pltpu.VMEM((terms, grids, per, strip, ny), f32),
+            pltpu.VMEM((nx, count, ny), f32),
+            pltpu.VMEM((nx, count, ny), f32),
+            pltpu.VMEM((count * half, 3 * ranks), jnp.bfloat16),
+            pltpu.VMEM((nx, ys, 2, rows, ny), f32),
+            pltpu.VMEM((nx, ranks, ny), f32),
+            pltpu.VMEM((2, nx, ys, 2, rows, ny), f32),
+            pltpu.VMEM((nx, half, ny), f32),
+            pltpu.VMEM((nx, half, ny), f32),
+            pltpu.VMEM((2, 8, 128), f32),
+            dma((grids * ys,)), dma((grids * ys,)),
+            dma((grids * ys,)), dma((grids * ys,)),
+            dma((terms,)), dma((terms,)),
+            dma((terms,)), dma((terms,)),
+            dma((grids * terms,)), dma((grids * terms,)),
+            dma((2, nx)), dma((2, nx)),
+            dma, dma,
+        ],
+        compiler_params=pltpu.CompilerParams(
+            collective_id=0, has_side_effects=True, vmem_limit_bytes=48 * 2**20
+        ),
+    )(rhs, coef, env)
+    return sol.transpose(1, 0, 2), res.transpose(1, 0, 2)
+
+
+def fits(mesh, rhs):
+    cells = rhs.shape[1] * mesh.shape["grid"] * rhs.shape[2]
+    return mesh.shape["rank"] == 4 and rhs.shape[0] * 4 * cells * 4 <= 2**20
+
+
 def solution(mesh):
     placed = (P("rank", "grid", None), P("term", "grid", None), P("term", "rank", None))
+
+    def run(rhs, coef, env):
+        if fits(mesh, rhs):
+            return fused(mesh, rhs, coef, env)
+        return shards(rhs, coef, env)
+
     return jax.shard_map(
-        shards,
+        run,
         mesh=mesh,
         in_specs=placed,
         out_specs=(P("rank", "grid", None), P("rank", "grid", None)),

time: 444 us -> 36 us (0.08)
  waiting for transfers between devices: 280 us -> 0 us
  blocking collectives: 87.3 us -> 0 us
  Pallas kernels: 0 us -> 31.4 us
  starting transfers between devices: 26.2 us -> 0 us
  between operations: 24.8 us -> 0.65 us
  local copies, waits for them, and re-layouts: 13.1 us -> 3.68 us
  other arithmetic: 9.37 us -> 0 us
    psum x4 -> x0, waiting for transfers between devices: 142 us -> none  [shards(): image = lax.psum(image, 'term')]
    unnamed x12 -> x0, waiting for transfers between devices: 121 us -> none
    psum x7 -> x0, blocking collectives: 87.3 us -> none  [the longest x4 49.9 us: square_sum(): return lax.psum(jnp.sum(vector * vector), ('grid', 'rank'))]
    pallas_call x0 -> x1, Pallas kernels: none -> 31.4 us  [fused(): pl.pallas_call(functools.partial(cg_kernel, sizes), out_shape=(block, blo...]
    ppermute x10 -> x0, starting transfers between devices: 25.9 us -> none  [the longest x5 19.4 us: padded_2(): lax.ppermute(lax.slice_in_dim(block, block.shape[dim] - width, None, axis...]
    ppermute x10 -> x0, waiting for transfers between devices: 17.7 us -> none  [the longest x5 16.9 us: padded_2(): lax.ppermute(lax.slice_in_dim(block, 0, width, axis=dim), axis, backward)]
    reduce_sum x7 -> x0, other arithmetic: 8.34 us -> none  [the longest x4 6.33 us: shards(): alpha = norm_now / lax.psum(jnp.sum(direction * image), ('grid', 'rank'))]
  transfers between devices with their start and end apart: 18 -> 0, of which waited for: 15 -> 0; matrix products, arithmetic and copies ran while one was open for 0% -> 0% of each run, Pallas kernels for 0% -> 0%
where the time goes in v1:
time: 36 us; the launch traced here: 35.8 us
  Pallas kernels  31.4 us (87%)
  local copies, waits for them, and re-layouts  3.68 us (10%)
  between operations  0.65 us (2%)
    pallas_call x1, Pallas kernels, fused(): pl.pallas_call(functools.partial(cg_kernel, sizes), out_shape=(block, blo...  31.4 us
    unnamed x8, local copies, waits for them, and re-layouts  3.68 us

profile of v1, /device:TPU:0, one launch (start us, length us, event | category | flops | bytes accessed | tf_op | source)
XLA Modules:
  0.0 35.8 jit_solution(12071009039350614165)
XLA Ops:
  0.6 0.0 copy-start
  0.6 0.8 %copy-done = f32[32,2,256]{2,1,0:T(2,128)S(1)} copy-done((f32[32,2,256]{2,1,0:T(2,128)S(1)}, f32[32,2,256]{2,1,0:T(2,128)}, u32[]{:S(2)}) %copy-start) | copy-done | bytes 65560
  1.5 0.0 copy-start.1
  1.5 0.8 %copy-done.1 = f32[3,32,128]{2,1,0:T(8,128)S(1)} copy-done((f32[3,32,128]{2,1,0:T(8,128)S(1)}, f32[3,32,128]{2,1,0:T(8,128)}, u32[]{:S(2)}) %copy-start.1) | copy-done | bytes 49176
  2.3 0.0 copy-start.2
  2.3 0.7 %copy-done.2 = f32[3,2,256]{2,1,0:T(2,128)S(1)} copy-done((f32[3,2,256]{2,1,0:T(2,128)S(1)}, f32[3,2,256]{2,1,0:T(2,128)}, u32[]{:S(2)}) %copy-start.2) | copy-done | bytes 6168
  3.0 31.4 %shard_map.50 = (f32[2,32,256]{2,1,0:T(8,128)S(1)}, f32[2,32,256]{2,1,0:T(8,128)S(1)}) custom-call(f32[32,2,256]{2,1,0:T(2,128)S(1)} %copy-done, f32[3,2,256]{2,1,0:T(2,128)S(1)} %copy-done.2, f32[3,32,128]{2,1,0:T(8,128)S(1)} %copy-done.1), custom_call_target="tpu_custom_call" | custom-call | tf_op jit(solution)/shard_map/pallas_call | solution.py:323
  34.4 0.7 %copy.5 = f32[32,2,256]{2,1,0:T(2,128)} copy(f32[32,2,256]{2,0,1:T(8,128)S(1)} %bitcast.3) | data formatting | bytes 131072
  35.1 0.7 %copy.6 = f32[32,2,256]{2,1,0:T(2,128)} copy(f32[32,2,256]{2,0,1:T(8,128)S(1)} %bitcast.2) | data formatting | bytes 131072
Async XLA Ops:
  0.6 0.8 %copy-start = (f32[32,2,256]{2,1,0:T(2,128)S(1)}, f32[32,2,256]{2,1,0:T(2,128)}, u32[]{:S(2)}) copy-start(f32[32,2,256]{2,1,0:T(2,128)} %rhs_ref.1) | copy-start | bytes 196612
  1.5 0.8 %copy-start.1 = (f32[3,32,128]{2,1,0:T(8,128)S(1)}, f32[3,32,128]{2,1,0:T(8,128)}, u32[]{:S(2)}) copy-start(f32[3,32,128]{2,1,0:T(8,128)} %env_ref.1) | copy-start | bytes 147460
  2.3 0.7 %copy-start.2 = (f32[3,2,256]{2,1,0:T(2,128)S(1)}, f32[3,2,256]{2,1,0:T(2,128)}, u32[]{:S(2)}) copy-start(f32[3,2,256]{2,1,0:T(2,128)} %coef_ref.1) | copy-start | bytes 18436

commit v2 on v1

--- a/solution.py
+++ b/solution.py
@@ -109,11 +109,12 @@
     sizes,
     rhs_ref, coef_ref, env_ref,
     sol_ref, out_ref,
-    env_all, coef_all, coef_tab, diag_tab, stack, residual, direction, image, partial, weighted, dots,
-    rhs_send, rhs_recv, sib_send, sib_recv, env_send, env_recv, envy_send, envy_recv,
+    rhs_own, env_all, coef_all, coef_tab, diag_tab, stack, residual, direction, image, partial, weighted, dots,
+    load, rhs_send, rhs_recv, sib_send, sib_recv, env_send, env_recv, envy_send, envy_recv,
     coef_send, coef_recv, img_send, img_recv, dot_send, dot_recv,
 ):
-    grids, ys, terms, per, rows, strip, ny, ranks = sizes
+    terms, per, rows, strip, ny, ranks = sizes
+    grids, ys = 2, 2
     nx = grids * strip
     half = ys * rows
     gx = lax.axis_index("grid")
@@ -123,77 +124,103 @@
     core = rank % 2
     sibling = (gx, gy * 2 + (1 - core), gz)
 
-    def at(dx, dy, dz):
-        return ((gx + dx) % grids, ((gy + dy) % ys) * 2 + core, (gz + dz) % terms)
-
-    peers = [at(dx, 0, dz) for dx in range(grids) for dz in range(terms) if dx or dz]
-    peers += [at(dx, dy, 0) for dx in range(grids) for dy in range(1, ys)]
-    peers.append(sibling)
+    def at(x, y, z):
+        return (x, y * 2 + core, z)
+
+    origins = [gz + 1 - 2 * (gz % 2), 2 - gz // 2, 3 - 3 * (gz // 2)]
+    over_x, over_y, across = at(1 - gx, gy, gz), at(gx, 1 - gy, gz), at(1 - gx, 1 - gy, gz)
+    line = [at(gx, gy, o) for o in origins]
+
+    loads = [
+        pltpu.make_async_copy(rhs_ref, rhs_own, load.at[0]),
+        pltpu.make_async_copy(env_ref, env_all.at[gz, :, gy], load.at[1]),
+        pltpu.make_async_copy(coef_ref, coef_all.at[gz, gx], load.at[2]),
+    ]
+    for copy in loads:
+        copy.start()
+
     barrier = pltpu.get_barrier_semaphore()
+
+    def greet(peer):
+        pl.semaphore_signal(barrier, inc=1, device_id=peer, device_id_type=MESH)
+
+    peers = line + [over_x, over_y, across, sibling]
     for peer in peers:
-        pl.semaphore_signal(barrier, inc=1, device_id=peer, device_id_type=MESH)
-
+        greet(peer)
+
+    loads[0].wait()
     for i in range(strip):
-        residual[gx * strip + i, gy, core] = rhs_ref[:, i, :]
-    env_all[gz, :, gy] = env_ref[...]
-    coef_all[gz, gx] = coef_ref[...]
+        residual[gx * strip + i, gy, core] = rhs_own[:, i, :]
+    loads[1].wait()
+    loads[2].wait()
     pl.semaphore_wait(barrier, len(peers))
 
+    sent = []
+
     def remote(src, dst, send, recv, device):
-        copy = pltpu.make_async_remote_copy(
+        return pltpu.make_async_remote_copy(
             src_ref=src, dst_ref=dst, send_sem=send, recv_sem=recv, device_id=device, device_id_type=MESH
         )
+
+    def push(block, send, recv, device):
+        copy = remote(block, block, send, recv, device)
+        sent.append(copy)
+        copy.start()
         return copy
 
-    def block_of(dx, dy, which):
-        return residual.at[pl.ds(((gx + dx) % grids) * strip, strip), (gy + dy) % ys, which]
-
-    own = block_of(0, 0, core)
-    env_copies, envy_copies, rhs_copies, sib_copies, coef_copies = {}, {}, {}, {}, {}
-    order = [1, terms - 1] + list(range(2, terms - 1))
-    for dz in order:
-        copy = remote(env_ref, env_all.at[gz, :, gy], env_send.at[dz], env_recv.at[dz], at(0, 0, dz))
-        copy.start()
-        env_copies[dz] = copy
-    for dx in range(grids):
-        for dy in range(ys):
-            if dx or dy:
-                d = dx * ys + dy
-                copy = remote(own, own, rhs_send.at[d], rhs_recv.at[d], at(dx, dy, 0))
-                copy.start()
-                rhs_copies[d] = copy
-    envy_copies[0] = remote(env_ref, env_all.at[gz, :, gy], envy_send.at[0], envy_recv.at[0], at(0, 1, 0))
-    envy_copies[0].start()
-    for dx in range(grids):
-        for dz in range(terms):
-            if dx or dz:
-                d = dx * terms + dz
-                copy = remote(coef_ref, coef_all.at[gz, gx], coef_send.at[d], coef_recv.at[d], at(dx, 0, dz))
-                copy.start()
-                coef_copies[d] = copy
-
-    def to_sibling(dx, dy):
-        d = dx * ys + dy
-        block = block_of(dx, dy, core)
-        copy = remote(block, block, sib_send.at[d], sib_recv.at[d], sibling)
-        copy.start()
-        sib_copies[d] = copy
-
-    to_sibling(0, 0)
-    for dx in range(grids):
-        for dy in range(ys):
-            if dx or dy:
-                rhs_copies[dx * ys + dy].wait_recv()
-                to_sibling(dx, dy)
-    for dz in order:
-        env_copies[dz].wait_recv()
-        block = env_all.at[(gz - dz + terms) % terms, :, gy]
-        copy = remote(block, block, envy_send.at[dz], envy_recv.at[dz], at(0, 1, 0))
-        copy.start()
-        envy_copies[dz] = copy
-
-    for copy in coef_copies.values():
+    def arrived(block, recv):
+        remote(block, block, dot_send, recv, sibling).wait_recv()
+
+    def strip_of(x, y):
+        return residual.at[pl.ds(x * strip, strip), y, core]
+
+    def env_line(o):
+        return env_all.at[o, :, gy]
+
+    own = strip_of(gx, gy)
+    for i in (2, 1, 0):
+        push(env_line(gz), env_send.at[i], env_recv.at[gz], line[i])
+    rhs_y = push(own, rhs_send.at[0], rhs_recv.at[0], over_y)
+    rhs_x = push(own, rhs_send.at[1], rhs_recv.at[1], over_x)
+    rhs_d = push(own, rhs_send.at[2], rhs_recv.at[2], across)
+    for i in (2, 1, 0):
+        push(coef_all.at[gz, gx], coef_send.at[i], coef_recv.at[gz], line[i])
+    push(env_line(gz), envy_send.at[3], envy_recv.at[gz], over_y)
+    sibs = [push(own, sib_send.at[0], sib_recv.at[0], sibling)]
+
+    def put_stack(o):
+        for i in range(per):
+            block = env_all[o, i].reshape(half, ranks)
+            high = block.astype(jnp.bfloat16)
+            low = (block - high.astype(jnp.float32)).astype(jnp.bfloat16)
+            at = pl.ds(pl.multiple_of((o * per + i) * half, half), half)
+            stack[at, 0:ranks] = high
+            stack[at, ranks : 2 * ranks] = low
+            stack[at, 2 * ranks : 3 * ranks] = high
+
+    def cross(i):
+        o = origins[i]
+        arrived(env_line(o), env_recv.at[o])
+        push(env_line(o), envy_send.at[i], envy_recv.at[o], over_y)
+
+    def to_sibling(i, copy, x, y):
         copy.wait_recv()
+        sibs.append(push(strip_of(x, y), sib_send.at[i], sib_recv.at[i], sibling))
+
+    def crossed_into_stack(o):
+        arrived(env_all.at[o, :, 1 - gy], envy_recv.at[o])
+        put_stack(o)
+
+    cross(0)
+    to_sibling(1, rhs_y, gx, 1 - gy)
+    to_sibling(2, rhs_x, 1 - gx, gy)
+    to_sibling(3, rhs_d, 1 - gx, 1 - gy)
+    cross(1)
+    for o in origins:
+        arrived(coef_all.at[o, gx], coef_recv.at[o])
+    coef_x = push(coef_all.at[:, gx], coef_send.at[terms - 1], coef_recv.at[gz], over_x)
+    cross(2)
+    coef_x.wait_recv()
     for x in range(nx):
         for z in range(terms):
             for i in range(per):
@@ -201,8 +228,7 @@
                 coef_tab[x, k : k + 1, :] = coef_all[z, x // strip, i, x % strip : x % strip + 1, :]
     for x in range(nx):
         diag_tab[x] = 0.5 * neighbours(lambda j: coef_tab[j], x, nx)
-
-    for copy in sib_copies.values():
+    for copy in sibs:
         copy.wait_recv()
     square = jnp.zeros((ranks, ny), jnp.float32)
     for x in range(nx):
@@ -210,21 +236,10 @@
         direction[x] = field
         square = square + field * field
     norm_now = total_sum(square)
-
-    for copy in envy_copies.values():
-        copy.wait_recv()
-    for z in range(terms):
-        for i in range(per):
-            k = z * per + i
-            block = env_all[z, i].reshape(half, ranks)
-            high = block.astype(jnp.bfloat16)
-            low = (block - high.astype(jnp.float32)).astype(jnp.bfloat16)
-            stack[pl.ds(k * half, half), 0:ranks] = high
-            stack[pl.ds(k * half, half), ranks : 2 * ranks] = low
-            stack[pl.ds(k * half, half), 2 * ranks : 3 * ranks] = high
-    for copies in (env_copies, envy_copies, rhs_copies, sib_copies, coef_copies):
-        for copy in copies.values():
-            copy.wait_send()
+    for o in [gz] + origins:
+        crossed_into_stack(o)
+    for copy in sent:
+        copy.wait_send()
 
     count = terms * per
 
@@ -311,21 +326,22 @@
 
 
 def fused(mesh, rhs, coef, env):
-    grids, rank_shards, terms = (mesh.shape[a] for a in ("grid", "rank", "term"))
-    ys = rank_shards // 2
+    terms = mesh.shape["term"]
     rows, strip, ny = rhs.shape
     per, ranks = env.shape[0], env.shape[2]
+    grids, ys = 2, 2
     nx, half, count = grids * strip, ys * rows, per * terms
-    sizes = (grids, ys, terms, per, rows, strip, ny, ranks)
+    sizes = (terms, per, rows, strip, ny, ranks)
     f32 = jnp.float32
     dma = pltpu.SemaphoreType.DMA
     block = jax.ShapeDtypeStruct((strip, rows, ny), f32)
     sol, res = pl.pallas_call(
         functools.partial(cg_kernel, sizes),
         out_shape=(block, block),
-        in_specs=[pl.BlockSpec(memory_space=pltpu.VMEM)] * 3,
+        in_specs=[pl.BlockSpec(memory_space=pltpu.HBM)] * 3,
         out_specs=(pl.BlockSpec(memory_space=pltpu.VMEM),) * 2,
         scratch_shapes=[
+            pltpu.VMEM((rows, strip, ny), f32),
             pltpu.VMEM((terms, per, ys, rows, ranks), f32),
             pltpu.VMEM((terms, grids, per, strip, ny), f32),
             pltpu.VMEM((nx, count, ny), f32),
@@ -337,16 +353,17 @@
             pltpu.VMEM((nx, half, ny), f32),
             pltpu.VMEM((nx, half, ny), f32),
             pltpu.VMEM((2, 8, 128), f32),
-            dma((grids * ys,)), dma((grids * ys,)),
-            dma((grids * ys,)), dma((grids * ys,)),
+            dma((3,)),
+            dma((3,)), dma((3,)),
+            dma((4,)), dma((4,)),
+            dma((terms - 1,)), dma((terms,)),
             dma((terms,)), dma((terms,)),
             dma((terms,)), dma((terms,)),
-            dma((grids * terms,)), dma((grids * terms,)),
             dma((2, nx)), dma((2, nx)),
             dma, dma,
         ],
         compiler_params=pltpu.CompilerParams(
-            collective_id=0, has_side_effects=True, vmem_limit_bytes=48 * 2**20
+            collective_id=0, has_side_effects=True, vmem_limit_bytes=63 * 2**20
         ),
     )(rhs, coef, env)
     return sol.transpose(1, 0, 2), res.transpose(1, 0, 2)
@@ -354,7 +371,7 @@
 
 def fits(mesh, rhs):
     cells = rhs.shape[1] * mesh.shape["grid"] * rhs.shape[2]
-    return mesh.shape["rank"] == 4 and rhs.shape[0] * 4 * cells * 4 <= 2**20
+    return mesh.shape["rank"] == 4 and mesh.shape["grid"] == 2 and mesh.shape["term"] == 4 and rhs.shape[0] * 4 * cells * 4 <= 2**20
 
 
 def solution(mesh):

time: 36 us -> 34 us (0.944)
  local copies, waits for them, and re-layouts: 3.68 us -> 2.24 us
  Pallas kernels: 31.4 us -> 30.9 us
    unnamed x8 -> x4, local copies, waits for them, and re-layouts: 3.68 us -> 2.24 us
    pallas_call x1, Pallas kernels: 31.4 us -> 30.9 us  [fused(): pl.pallas_call(functools.partial(cg_kernel, sizes), out_shape=(block, blo...]
where the time goes in v2:
time: 34 us; the launch traced here: 33.7 us
  Pallas kernels  30.9 us (91%)
  local copies, waits for them, and re-layouts  2.24 us (7%)
  between operations  0.65 us (2%)
    pallas_call x1, Pallas kernels, fused(): pl.pallas_call(functools.partial(cg_kernel, sizes), out_shape=(block, blo...  30.9 us
    unnamed x4, local copies, waits for them, and re-layouts  2.24 us

profile of v2, /device:TPU:0, one launch (start us, length us, event | category | flops | bytes accessed | tf_op | source)
XLA Modules:
  0.0 33.7 jit_solution(14895144900021486737)
XLA Ops:
  0.6 30.9 %shard_map.50 = (f32[2,32,256]{2,1,0:T(8,128)}, f32[2,32,256]{2,1,0:T(8,128)}) custom-call(f32[32,2,256]{2,1,0:T(2,128)} %rhs_ref.1, f32[3,2,256]{2,1,0:T(2,128)} %coef_ref.1, f32[3,32,128]{2,1,0:T(8,128)} %env_ref.1), custom_call_target="tpu_custom_call" | custom-call | tf_op jit(solution)/shard_map/pallas_call | solution.py:338
  31.5 0.0 copy-start
  31.5 1.6 %copy.5 = f32[32,2,256]{2,1,0:T(2,128)} copy(f32[32,2,256]{2,0,1:T(8,128)} %bitcast.3) | data formatting | bytes 131072
  33.1 0.0 copy-done
  33.1 0.7 %copy.6 = f32[32,2,256]{2,1,0:T(2,128)} copy(f32[32,2,256]{2,0,1:T(8,128)S(1)} %bitcast.2) | data formatting | bytes 131072
Async XLA Ops:
  31.5 1.6 %copy-start = (f32[2,32,256]{2,1,0:T(8,128)S(1)}, f32[2,32,256]{2,1,0:T(8,128)}, u32[]{:S(2)}) copy-start(f32[2,32,256]{2,1,0:T(8,128)} %get-tuple-element.5) | copy-start | bytes 196612
